TPU v7x, 32 devices: a whole 2x2x4 slice. The times are simulated.
32 devices in a mesh: row: 8 (over z, x), col: 4 (over y, core).
Axes of the slice: x: 2, y: 2, z: 4, core: 2. Of those that a mesh axis runs over, the one named last changes fastest.
Arguments:
- factor: float32 [2, 2048, 2, 1024], P(None, 'row', None, 'col'), may hold values from -5 to 5, as said below
- update: float32 [2, 2048, 512], P(None, 'row', 'col'), may hold values from -1.5 to 1.5
Outputs:
- updated_factor: float32 [2, 2048, 2, 1024], P(None, 'row', None, 'col')
Inputs may be any that keep to these rules, and one draw needn't show every extreme that they name: `factor`: in the first 2048 rows, entries to the right of the diagonal are zero and diagonal entries are positive.
All inputs are finite; a program needn't handle non-finite values.
Results may differ from a plain program's by a relative error of at most 0.0003.
Values sent between devices are 32-bit elements; how exact they have to be, the bound alone decides.
A program may use at most 128 MiB of HBM per device.

v0:
```python
import functools

import jax
import jax.numpy as jnp
from jax import lax
from jax.experimental import pallas as pl
from jax.experimental.pallas import tpu as pltpu
from jax.sharding import PartitionSpec as P

PANEL = 1024
PANELS = 2
B=256; H=128; GRP=8
NN=(((1,),(0,)),((),()))
NT=(((1,),(1,)),((),())); TN=(((0,),(0,)),((),()))
def split(x):
    hi=x.astype(jnp.bfloat16); return hi,(x-hi.astype(jnp.float32)).astype(jnp.bfloat16)
def dot3(a,b,dims=NT):
    (ah,al),(bh,bl)=a,b
    d=functools.partial(lax.dot_general,dimension_numbers=dims,preferred_element_type=jnp.float32)
    return d(ah,bh)+(d(ah,bl)+d(al,bh))
def small(a,b,dims=NT):
    return dot3(split(a),split(b),dims)
def factor_half(s_ref, a):
    rows=lax.broadcasted_iota(jnp.int32,(H,H),0); cols=lax.broadcasted_iota(jnp.int32,(H,H),1)
    s_ref[:, :H]=a
    s_ref[:, H:]=(rows==cols).astype(jnp.float32)
    sub=lax.broadcasted_iota(jnp.int32,(GRP,1),0)
    for g in range(H//GRP):
        j=g*GRP
        r=s_ref[j:j+GRP,:]
        cb=[jnp.broadcast_to(r[:,j+b:j+b+1],(GRP,H)) for b in range(GRP)]
        for i in range(GRP):
            rs=lax.rsqrt(cb[i][i:i+1,:])
            m=jnp.where(sub>i,cb[i]*rs,0.0)
            rs2=jnp.concatenate([rs,rs],axis=1); m2=jnp.concatenate([m,m],axis=1)
            u=r[i:i+1,:]*rs2
            r=jnp.where(sub==i,u,r-m2*u)
            for b in range(i+1,GRP):
                cb[b]=cb[b]-m*(cb[b][i:i+1,:]*rs)
        s_ref[j:j+GRP,:]=r
        if j+GRP<H:
            s_ref[j+GRP:,:]=s_ref[j+GRP:,:]-small(r[:,j+GRP:H],r,TN)
    u=jnp.where(rows<=cols,s_ref[:, :H],0.0)
    return u, s_ref[:, H:]

def factor_panel(nrow, ncol, g, ph, plo, inv, s_ref):
    def step(k, _):
        kc = pl.ds(pl.multiple_of(k * B, B), B)
        a = g[k, :, kc]
        u1, v1 = factor_half(s_ref, a[:H, :H])
        l21 = small(a[H:, :H], v1, NT)
        u2, v2 = factor_half(s_ref, a[H:, H:] - small(l21, l21, NT))
        zero = jnp.zeros((H, H), jnp.float32)
        inv[:H, :H] = v1
        inv[:H, H:] = zero
        inv[H:, :H] = -small(v2, small(l21, v1, NN), NN)
        inv[H:, H:] = v2
        g[k, :H, kc] = jnp.concatenate([u1.T, zero], axis=1)
        g[k, H:, kc] = jnp.concatenate([l21, u2.T], axis=1)
        iv = split(inv[...])

        def panel(i, _):
            p = dot3(split(g[i, :, kc]), iv)
            g[i, :, kc] = p
            ph[i], plo[i] = split(p)
            return 0

        lax.fori_loop(k + 1, nrow, panel, 0)

        def colup(j, _):
            jc = pl.ds(pl.multiple_of(j * B, B), B)
            w = (ph[j], plo[j])

            def rowup(i, _):
                g[i, :, jc] = g[i, :, jc] - dot3((ph[i], plo[i]), w)
                return 0

            lax.fori_loop(j, nrow, rowup, 0)
            return 0

        lax.fori_loop(k + 1, ncol, colup, 0)
        return 0

    lax.fori_loop(0, ncol, step, 0)


def panel_kernel(p, ntile, nown, sizes, *refs):
    tc, uc, ncol_dev = sizes
    per = PANEL // B
    first = p * per
    nrow = ntile - first + nown
    if p == 0:
        idx, d_ref, o_ref, out_ref, f_out, xh, xl, g, ph, plo, inv, s_ref = refs
    else:
        idx, d_ref, o_ref, d1_ref, o1_ref, f_in, out_ref, xh, xl, g, ph, plo, inv, s_ref = refs
    width = PANEL + uc * ncol_dev
    for i in range(nrow):
        t = i + first
        src = d_ref if t < ntile else o_ref
        at = (i if p else t) if t < ntile else t - ntile
        for c in range(ncol_dev):
            xh[i, :, c * tc : (c + 1) * tc], xl[i, :, c * tc : (c + 1) * tc] = split(src[at, c, :, :tc])
            lo = PANEL + c * uc
            xh[i, :, lo : lo + uc], xl[i, :, lo : lo + uc] = split(src[at, c, :, tc:])
        if p:
            src = d1_ref if t < ntile else o1_ref
            for c in range(ncol_dev):
                lo = width + c * tc
                xh[i, :, lo : lo + tc], xl[i, :, lo : lo + tc] = split(src[at, c])
            xh[i, :, width + PANEL :], xl[i, :, width + PANEL :] = split(f_in[i])
    full = width + p * PANEL

    def gram_col(j, _):
        jc = pl.ds(pl.multiple_of(j * B, B), B)

        def gram_row(i, _):
            v = dot3((xh[i, :, :full], xl[i, :, :full]), (xh[j, :, :full], xl[j, :, :full]))
            if p:
                v = v - dot3((xh[i, :, full:], xl[i, :, full:]), (xh[j, :, full:], xl[j, :, full:]))
            g[i, :, jc] = v
            return 0

        lax.fori_loop(j, nrow, gram_row, 0)
        return 0

    lax.fori_loop(0, per, gram_col, 0)
    factor_panel(nrow, per, g, ph, plo, inv, s_ref)
    if p == 0:
        f_out[...] = g[per:]
    oc = pl.ds(pl.multiple_of(idx[1] * tc, tc), tc)
    if nown == 1:
        r = idx[0] - first
        t = g[jnp.maximum(r, 0), :, oc]
        keep = idx[1] * (tc // B) <= r
        out_ref[0] = jnp.where(keep, t, 0.0)
        out_ref[1] = g[nrow - 1, :, oc]
    else:
        for e in range(2):
            out_ref[e] = g[nrow - 2 + e, :, oc]


def run_panel(p, idx, ntile, nown, sizes, *arrays):
    tc, uc, nc = sizes
    per = PANEL // B
    nrow = ntile - p * per + nown
    width = PANEL + uc * nc + p * 2 * PANEL
    vm = pl.BlockSpec(memory_space=pltpu.VMEM)
    shape = [jax.ShapeDtypeStruct((2, B, tc), jnp.float32)]
    if p == 0:
        shape.append(jax.ShapeDtypeStruct((nrow - per, B, PANEL), jnp.float32))
    return pl.pallas_call(
        functools.partial(panel_kernel, p, ntile, nown, sizes),
        out_shape=shape,
        in_specs=[pl.BlockSpec(memory_space=pltpu.SMEM)] + [vm] * len(arrays),
        out_specs=[vm] * len(shape),
        scratch_shapes=[
            pltpu.VMEM((nrow, B, width), jnp.bfloat16),
            pltpu.VMEM((nrow, B, width), jnp.bfloat16),
            pltpu.VMEM((nrow, B, PANEL), jnp.float32),
            pltpu.VMEM((nrow, B, B), jnp.bfloat16),
            pltpu.VMEM((nrow, B, B), jnp.bfloat16),
            pltpu.VMEM((B, B), jnp.float32),
            pltpu.VMEM((H, 2 * H), jnp.float32),
        ],
        cost_estimate=pl.CostEstimate(flops=60_000_000_000, bytes_accessed=30_000_000, transcendentals=0),
        compiler_params=pltpu.CompilerParams(vmem_limit_bytes=60 * 2**20),
        name="panel%d" % p,
    )(idx, *arrays)


def per_device(factor, update):
    blocks, tile_rows, panels, tc = factor.shape
    uc = update.shape[2]
    nr, nc = lax.axis_size("row"), lax.axis_size("col")
    r, c = lax.axis_index("row"), lax.axis_index("col")
    ntile = PANELS * PANEL // tile_rows
    whole_rows = nr == ntile
    nown = blocks - 1 if whole_rows else blocks
    sizes = (tc, uc, nc)
    xa = jnp.concatenate([factor[:, :, 0], update], axis=2)
    xb = factor[:, :, 1]

    def diag(x):
        if whole_rows:
            return lax.all_gather(x, ("row", "col")).reshape(ntile, nc, *x.shape)
        tiles = [lax.psum(jnp.where(r == t, x, 0.0), "row") for t in range(ntile)]
        return jnp.moveaxis(lax.all_gather(jnp.stack(tiles), "col"), 0, 1)

    def own(x):
        return jnp.moveaxis(lax.all_gather(x[blocks - nown :], "col"), 0, 1)

    da, oa = diag(xa[0]), own(xa)
    xb = xb + (da[0, 0, 0, 0] + oa[0, 0, 0, 0]) * 0.0
    db, ob = diag(xb[0]), own(xb)
    idx = jnp.stack([r, c]).astype(jnp.int32)
    out0, f0 = run_panel(0, idx, ntile, nown, sizes, da, oa)
    (out1,) = run_panel(1, idx, ntile, nown, sizes, da[ntile // 2 :], oa, db[ntile // 2 :], ob, f0)
    out = jnp.stack([out0, out1], axis=2)
    if not whole_rows:
        rows = (
            jnp.arange(blocks)[:, None] * (nr * tile_rows) + r * tile_rows + jnp.arange(tile_rows)
        )
        cols = jnp.arange(panels)[:, None] * PANEL + c * tc + jnp.arange(tc)
        out = jnp.where(cols <= rows[:, :, None, None], out, 0.0)
    return out


def solution(mesh):
    in_specs = (P(None, "row", None, "col"), P(None, "row", "col"))
    out_specs = P(None, "row", None, "col")
    return jax.shard_map(
        per_device, mesh=mesh, in_specs=in_specs, out_specs=out_specs, check_vma=False
    )
```

profile of v0, /device:TPU:9, one launch (start us, length us, event | category | flops | bytes accessed | tf_op | source)
XLA Modules:
  0.0 361.6 jit_solution(5765250362775681341)
XLA Ops:
  6.5 0.0 all-gather.10.cloned.1.call-start
  6.5 2.6 fusion.1
  9.2 1.9 pad_maximum_fusion.1
  11.1 0.0 all-gather.10.cloned.1.call-update
  11.1 0.0 all-gather.8.cloned.1.call-start
  11.2 0.7 all-gather.8.cloned.1.call-update
  11.9 0.0 all-gather.12.cloned.1.call-start
  11.9 20.6 %all-gather.10.cloned.1.call-done = f32[4,256,384]{2,1,0:T(8,128)} async-done(((f32[1,256,384]{2,1,0:T(8,128)}), f32[4,256,384]{2,1,0:T(8,128)}) %all-gather.10.cloned.1.call-update) | async-done | bytes 1572880 | tf_op jit(solution)/shard_map/all_gather | solution.py:190
  32.5 1.2 slice.58
  33.7 97.1 %all-gather.8.cloned.1.call-done = f32[32,256,384]{2,1,0:T(8,128)} async-done(((f32[1,256,384]{2,1,0:T(8,128)}), f32[32,256,384]{2,1,0:T(8,128)}) %all-gather.8.cloned.1.call-update) | async-done | bytes 12582928 | tf_op jit(solution)/shard_map/all_gather | solution.py:185
  130.9 1.2 slice.57
  133.4 0.8 fusion.2
  134.2 0.0 all-gather.12.cloned.1.call-update
  134.2 0.0 all-gather.14.cloned.1.call-start
  134.3 0.6 pad_add_fusion.refs_0_
  134.9 0.0 all-gather.14.cloned.1.call-update
  134.9 110.3 %panel0.1 = (f32[2,256,256]{2,1,0:T(8,128)}, f32[5,256,1024]{2,1,0:T(8,128)}) custom-call(s32[2]{0:T(128)} %pad_add_fusion.refs_0_, f32[8,4,256,384]{3,2,1,0:T(8,128)} %bitcast.16, f32[1,4,256,384]{3,2,1,0:T(8,128)} %bitcast.21), custom_call_target="tpu_custom_call" | custom-call | flops 60000002048 | bytes 30000000 | tf_op jit(solution)/shard_map/panel0/pallas_call | solution.py:151
  245.2 6.0 %slice.56 = f32[16,256,384]{2,1,0:T(8,128)} slice(f32[32,256,384]{2,1,0:T(8,128)} %all-gather.8.cloned.1.call-done), slice={[16:32], [0:256], [0:384]} | slice | bytes 12582912 | tf_op jit(solution)/shard_map/slice | solution.py:197
  251.2 0.0 all-gather.12.cloned.1.call-done
  251.2 4.6 %slice.60 = f32[16,256,1,256]{3,1,2,0:T(8,128)} slice(f32[32,256,1,256]{3,1,2,0:T(8,128)} %all-gather.12.cloned.1.call-done), slice={[16:32], [0:256], [0:1], [0:256]} | slice | bytes 8388608 | tf_op jit(solution)/shard_map/slice | solution.py:197
  255.8 0.0 all-gather.14.cloned.1.call-done
  255.8 0.0 copy-start
  255.8 96.4 %panel1.1 = f32[2,256,256]{2,1,0:T(8,128)} custom-call(s32[2]{0:T(128)} %pad_add_fusion.refs_0_, f32[4,4,256,384]{3,2,1,0:T(8,128)} %bitcast.13, f32[1,4,256,384]{3,2,1,0:T(8,128)} %bitcast.22, f32[4,4,256,256]{3,2,1,0:T(8,128)} %bitcast.14, f32[1,4,256,256]{3,2,1,0:T(8,128)} %bitcast.23, f32[5,256,1024]{2,1,0:T(8,128)} %get-tuple-element.8.refs_5_), custom_call_target="tpu_custom_call" | custom-call | flops 60000002048 | bytes 30000000 | tf_op jit(solution)/shard_map/panel1/pallas_call | solution.py:151
  352.1 0.0 copy-done
  352.1 1.1 pad_maximum_fusion
  353.3 1.8 copy.8
  (2 shorter events, 0.1 us)
Async XLA Ops:
  6.5 26.0 %all-gather.10.cloned.1.call-start = ((), (), s32[]{:S(2)}) async-start(), calls=%async_computation.1 | async-start | bytes 1966080 | tf_op jit(solution)/shard_map/all_gather | solution.py:190
  11.1 119.7 %all-gather.8.cloned.1.call-start = ((), (), s32[]{:S(2)}) async-start(), calls=%async_computation | async-start | bytes 12976128 | tf_op jit(solution)/shard_map/all_gather | solution.py:185
  11.9 239.3 %all-gather.12.cloned.1.call-start = ((), (), s32[]{:S(2)}) async-start(), calls=%async_computation.2 | async-start | bytes 8650752 | tf_op jit(solution)/shard_map/all_gather | solution.py:185
  134.2 121.5 %all-gather.14.cloned.1.call-start = ((), (), s32[]{:S(2)}) async-start(), calls=%async_computation.3 | async-start | bytes 1310720 | tf_op jit(solution)/shard_map/all_gather | solution.py:190
  255.8 96.4 %copy-start = (f32[2,256,256]{2,1,0:T(8,128)S(1)}, f32[2,256,256]{2,1,0:T(8,128)}, u32[]{:S(2)}) copy-start(f32[2,256,256]{2,1,0:T(8,128)} %get-tuple-element.7) | copy-start | bytes 1572868
Sparse Core Ops, SparseCore 0:
  11.3 21.2 all-gather.9
  35.4 95.4 all-gather.7
  134.4 77.1 all-gather.11
  213.0 15.6 all-gather.13
where the time goes:
time: 364 us; the launch traced here: 362 us
  Pallas kernels  207 us (57%)
  waiting for transfers between devices  118 us (32%)
  local copies, waits for them, and re-layouts  18.2 us (5%)
  between operations  14.4 us (4%)
  other arithmetic  3.67 us (1%)
    pallas_call x2, Pallas kernels, run_panel(): pl.pallas_call(functools.partial(panel_kernel, p, ntile, nown, sizes), ou...  207 us
    all_gather x2, waiting for transfers between devices, diag(): return lax.all_gather(x, ('row', 'col')).reshape(ntile, nc, *x.shape)  97.1 us
    all_gather x2, waiting for transfers between devices, own(): return jnp.moveaxis(lax.all_gather(x[blocks - nown:], 'col'), 0, 1)  20.6 us
  transfers between devices with their start and end apart: 4, of which 2 were waited for; matrix products, arithmetic and copies ran while one was open for 3% of the time, Pallas kernels for 30%

commit v1 on v0

--- a/solution.py
+++ b/solution.py
@@ -9,7 +9,7 @@
 
 PANEL = 1024
 PANELS = 2
-B=256; H=128; GRP=8
+B=256; H=128; GRP=8; AHEAD=3
 NN=(((1,),(0,)),((),()))
 NT=(((1,),(1,)),((),())); TN=(((0,),(0,)),((),()))
 def split(x):
@@ -20,28 +20,57 @@
     return d(ah,bh)+(d(ah,bl)+d(al,bh))
 def small(a,b,dims=NT):
     return dot3(split(a),split(b),dims)
+def wide(x):
+    return jnp.broadcast_to(x, (GRP, H))
+
+
 def factor_half(s_ref, a):
-    rows=lax.broadcasted_iota(jnp.int32,(H,H),0); cols=lax.broadcasted_iota(jnp.int32,(H,H),1)
-    s_ref[:, :H]=a
-    s_ref[:, H:]=(rows==cols).astype(jnp.float32)
-    sub=lax.broadcasted_iota(jnp.int32,(GRP,1),0)
-    for g in range(H//GRP):
-        j=g*GRP
-        r=s_ref[j:j+GRP,:]
-        cb=[jnp.broadcast_to(r[:,j+b:j+b+1],(GRP,H)) for b in range(GRP)]
+    rows = lax.broadcasted_iota(jnp.int32, (H, H), 0)
+    cols = lax.broadcasted_iota(jnp.int32, (H, H), 1)
+    s_ref[:, :H] = a
+    s_ref[:, H:] = (rows == cols).astype(jnp.float32)
+    sub = lax.broadcasted_iota(jnp.int32, (GRP, 1), 0)
+    n = H // GRP
+    live = {}
+    ahead = None
+    for g in range(n):
+        j = g * GRP
+        near = range(g, min(g + AHEAD + 1, n))
+        for h in near:
+            if h not in live:
+                live[h] = [s_ref[h * GRP : (h + 1) * GRP, :H], s_ref[h * GRP : (h + 1) * GRP, H:]]
+        cb = {h: [wide(live[h][0][:, j + b : j + b + 1]) for b in range(GRP)] for h in near if h > g or ahead is None}
+        if ahead is not None:
+            cb[g] = ahead
+        ahead = None
+        if g + 1 < n:
+            ahead = [wide(live[g + 1][0][:, j + GRP + b : j + GRP + b + 1]) for b in range(GRP)]
+        scale = None
         for i in range(GRP):
-            rs=lax.rsqrt(cb[i][i:i+1,:])
-            m=jnp.where(sub>i,cb[i]*rs,0.0)
-            rs2=jnp.concatenate([rs,rs],axis=1); m2=jnp.concatenate([m,m],axis=1)
-            u=r[i:i+1,:]*rs2
-            r=jnp.where(sub==i,u,r-m2*u)
-            for b in range(i+1,GRP):
-                cb[b]=cb[b]-m*(cb[b][i:i+1,:]*rs)
-        s_ref[j:j+GRP,:]=r
-        if j+GRP<H:
-            s_ref[j+GRP:,:]=s_ref[j+GRP:,:]-small(r[:,j+GRP:H],r,TN)
-    u=jnp.where(rows<=cols,s_ref[:, :H],0.0)
+            piv = [wide(cb[g][b][i : i + 1, :]) for b in range(i, GRP)]
+            rs = lax.rsqrt(piv[0])
+            inv = rs * rs
+            scale = rs if scale is None else jnp.where(sub == i, rs, scale)
+            u = [wide(x[i : i + 1, :]) for x in live[g]]
+            for h in near:
+                p = cb[h][i]
+                if h == g:
+                    p = jnp.where(sub > i, p, 0.0)
+                m = p * inv
+                live[h] = [x - m * y for x, y in zip(live[h], u)]
+                for b in range(i + 1, GRP):
+                    cb[h][b] = cb[h][b] - (p * piv[b - i]) * inv
+                if h == g + 1:
+                    ahead = [x - m * wide(p[b : b + 1, :]) for b, x in enumerate(ahead)]
+        done = [x * scale for x in live.pop(g)]
+        s_ref[j : j + GRP, :H], s_ref[j : j + GRP, H:] = done
+        lo = (g + AHEAD + 1) * GRP
+        if lo < H:
+            r = jnp.concatenate(done, axis=1)
+            s_ref[lo:, :] = s_ref[lo:, :] - small(r[:, lo:H], r, TN)
+    u = jnp.where(rows <= cols, s_ref[:, :H], 0.0)
     return u, s_ref[:, H:]
+
 
 def factor_panel(nrow, ncol, g, ph, plo, inv, s_ref):
     def step(k, _):

time: 364 us -> 307 us (0.84)
  Pallas kernels: 207 us -> 150 us
    pallas_call x2, Pallas kernels: 207 us -> 150 us  [run_panel(): pl.pallas_call(functools.partial(panel_kernel, p, ntile, nown, sizes), ou...]
  transfers between devices with their start and end apart: 4 -> 4, of which waited for: 2 -> 2; matrix products, arithmetic and copies ran while one was open for 3% -> 4% of each run, Pallas kernels for 30% -> 27%
where the time goes in v1:
time: 307 us; the launch traced here: 305 us
  Pallas kernels  150 us (49%)
  waiting for transfers between devices  118 us (38%)
  local copies, waits for them, and re-layouts  18.4 us (6%)
  between operations  14.4 us (5%)
  other arithmetic  3.67 us (1%)
    pallas_call x2, Pallas kernels, run_panel(): pl.pallas_call(functools.partial(panel_kernel, p, ntile, nown, sizes), ou...  150 us
    all_gather x2, waiting for transfers between devices, diag(): return lax.all_gather(x, ('row', 'col')).reshape(ntile, nc, *x.shape)  97.1 us
    all_gather x2, waiting for transfers between devices, own(): return jnp.moveaxis(lax.all_gather(x[blocks - nown:], 'col'), 0, 1)  20.6 us
    slice x1, local copies, waits for them, and re-layouts, per_device(): da[ntile // 2:]  6.3 us
  transfers between devices with their start and end apart: 4, of which 2 were waited for; matrix products, arithmetic and copies ran while one was open for 4% of the time, Pallas kernels for 27%

profile of v1, /device:TPU:9, one launch (start us, length us, event | category | flops | bytes accessed | tf_op | source)
XLA Modules:
  0.0 305.5 jit_solution(16984253780231348015)
XLA Ops:
  6.5 0.0 all-gather.10.cloned.1.call-start
  6.5 2.5 fusion.1
  9.1 1.9 pad_maximum_fusion.1
  11.0 0.0 all-gather.10.cloned.1.call-update
  11.0 0.0 all-gather.8.cloned.1.call-start
  11.1 0.7 all-gather.8.cloned.1.call-update
  11.8 0.0 all-gather.12.cloned.1.call-start
  11.8 20.6 %all-gather.10.cloned.1.call-done = f32[4,256,384]{2,1,0:T(8,128)} async-done(((f32[1,256,384]{2,1,0:T(8,128)}), f32[4,256,384]{2,1,0:T(8,128)}) %all-gather.10.cloned.1.call-update) | async-done | bytes 1572880 | tf_op jit(solution)/shard_map/all_gather | solution.py:219
  32.4 1.2 slice.58
  33.6 97.1 %all-gather.8.cloned.1.call-done = f32[32,256,384]{2,1,0:T(8,128)} async-done(((f32[1,256,384]{2,1,0:T(8,128)}), f32[32,256,384]{2,1,0:T(8,128)}) %all-gather.8.cloned.1.call-update) | async-done | bytes 12582928 | tf_op jit(solution)/shard_map/all_gather | solution.py:214
  130.8 1.2 slice.57
  133.3 0.8 fusion.2
  134.1 0.0 all-gather.12.cloned.1.call-update
  134.1 0.0 all-gather.14.cloned.1.call-start
  134.2 0.6 pad_add_fusion.refs_0_
  134.8 0.0 all-gather.14.cloned.1.call-update
  134.8 82.3 %panel0.1 = (f32[2,256,256]{2,1,0:T(8,128)}, f32[5,256,1024]{2,1,0:T(8,128)}) custom-call(s32[2]{0:T(128)} %pad_add_fusion.refs_0_, f32[8,4,256,384]{3,2,1,0:T(8,128)} %bitcast.16, f32[1,4,256,384]{3,2,1,0:T(8,128)} %bitcast.21), custom_call_target="tpu_custom_call" | custom-call | flops 60000002048 | bytes 30000000 | tf_op jit(solution)/shard_map/panel0/pallas_call | solution.py:180
  217.1 6.3 %slice.56 = f32[16,256,384]{2,1,0:T(8,128)} slice(f32[32,256,384]{2,1,0:T(8,128)} %all-gather.8.cloned.1.call-done), slice={[16:32], [0:256], [0:384]} | slice | bytes 12582912 | tf_op jit(solution)/shard_map/slice | solution.py:226
  223.3 0.0 all-gather.12.cloned.1.call-done
  223.3 4.6 %slice.60 = f32[16,256,1,256]{3,1,2,0:T(8,128)} slice(f32[32,256,1,256]{3,1,2,0:T(8,128)} %all-gather.12.cloned.1.call-done), slice={[16:32], [0:256], [0:1], [0:256]} | slice | bytes 8388608 | tf_op jit(solution)/shard_map/slice | solution.py:226
  227.9 0.0 all-gather.14.cloned.1.call-done
  227.9 0.0 copy-start
  227.9 68.1 %panel1.1 = f32[2,256,256]{2,1,0:T(8,128)} custom-call(s32[2]{0:T(128)} %pad_add_fusion.refs_0_, f32[4,4,256,384]{3,2,1,0:T(8,128)} %bitcast.13, f32[1,4,256,384]{3,2,1,0:T(8,128)} %bitcast.22, f32[4,4,256,256]{3,2,1,0:T(8,128)} %bitcast.14, f32[1,4,256,256]{3,2,1,0:T(8,128)} %bitcast.23, f32[5,256,1024]{2,1,0:T(8,128)} %get-tuple-element.8.refs_5_), custom_call_target="tpu_custom_call" | custom-call | flops 60000002048 | bytes 30000000 | tf_op jit(solution)/shard_map/panel1/pallas_call | solution.py:180
  296.0 0.0 copy-done
  296.0 1.1 pad_maximum_fusion
  297.2 1.8 copy.8
  (2 shorter events, 0.1 us)
Async XLA Ops:
  6.5 25.9 %all-gather.10.cloned.1.call-start = ((), (), s32[]{:S(2)}) async-start(), calls=%async_computation.1 | async-start | bytes 1966080 | tf_op jit(solution)/shard_map/all_gather | solution.py:219
  11.0 119.7 %all-gather.8.cloned.1.call-start = ((), (), s32[]{:S(2)}) async-start(), calls=%async_computation | async-start | bytes 12976128 | tf_op jit(solution)/shard_map/all_gather | solution.py:214
  11.8 211.5 %all-gather.12.cloned.1.call-start = ((), (), s32[]{:S(2)}) async-start(), calls=%async_computation.2 | async-start | bytes 8650752 | tf_op jit(solution)/shard_map/all_gather | solution.py:214
  134.1 93.8 %all-gather.14.cloned.1.call-start = ((), (), s32[]{:S(2)}) async-start(), calls=%async_computation.3 | async-start | bytes 1310720 | tf_op jit(solution)/shard_map/all_gather | solution.py:219
  227.9 68.1 %copy-start = (f32[2,256,256]{2,1,0:T(8,128)S(1)}, f32[2,256,256]{2,1,0:T(8,128)}, u32[]{:S(2)}) copy-start(f32[2,256,256]{2,1,0:T(8,128)} %get-tuple-element.7) | copy-start | bytes 1572868
Sparse Core Ops, SparseCore 0:
  11.2 21.2 all-gather.9
  35.3 95.4 all-gather.7
  134.3 76.5 all-gather.11
  212.2 15.2 all-gather.13

commit v2 on v1

--- a/solution.py
+++ b/solution.py
@@ -24,7 +24,7 @@
     return jnp.broadcast_to(x, (GRP, H))
 
 
-def factor_half(s_ref, a):
+def factor_half(s_ref, a, hook=None):
     rows = lax.broadcasted_iota(jnp.int32, (H, H), 0)
     cols = lax.broadcasted_iota(jnp.int32, (H, H), 1)
     s_ref[:, :H] = a
@@ -47,6 +47,8 @@
             ahead = [wide(live[g + 1][0][:, j + GRP + b : j + GRP + b + 1]) for b in range(GRP)]
         scale = None
         for i in range(GRP):
+            if hook is not None:
+                hook(g, i)
             piv = [wide(cb[g][b][i : i + 1, :]) for b in range(i, GRP)]
             rs = lax.rsqrt(piv[0])
             inv = rs * rs
@@ -166,6 +168,264 @@
     else:
         for e in range(2):
             out_ref[e] = g[nrow - 2 + e, :, oc]
+
+
+TASKS = 3
+NTOP = 8
+
+
+def tri(i, m):
+    return i * (i + 1) // 2 + m
+
+
+def xtile(i, m):
+    return 2 * (NTOP + 1) + tri(i, m)
+
+
+def ltile(i, m):
+    return 2 * (NTOP + 1) + tri(NTOP, NTOP) + i * (i - 1) // 2 + m
+
+
+NW = tri(NTOP, NTOP) + 1
+NPOOL = ltile(NTOP, NTOP)
+
+
+def plan(slots, late=()):
+    jobs = []
+    for i in range(NTOP + 1):
+        for m in range(min(i, NTOP - 1) + 1):
+            due = m if m < i else m - 1
+            for q in range(2):
+                jobs.append((due, 0, (tri(i, m), 2 * i + q, 2 * m + q, 1)))
+            for q in range(m + 1):
+                jobs.append((due, 0, (tri(i, m), xtile(i, q), xtile(m, q), 1)))
+            for q in range(m if m < i else m - 1):
+                jobs.append((due, q + 1, (tri(i, m), ltile(i, q), ltile(m, q), -1)))
+    first = [t for due, _, t in jobs if due < 0]
+    jobs = sorted((j for j in jobs if j[0] >= 0), key=lambda j: (j[0], -j[1]))
+    table = []
+    for k in range(NTOP):
+        now = [j for j in jobs if j[1] <= k][:slots]
+        jobs = [j for j in jobs if j not in now]
+        assert not jobs or jobs[0][0] > k
+        table += [t for _, _, t in now] + [(NW - 1, 0, 0, 1)] * (slots - len(now))
+    return first, table
+
+
+def split_into(ph, plo, t, x, lanes=slice(None)):
+    ph[t, :, lanes], plo[t, :, lanes] = split(x)
+
+
+def top_kernel(slots, first, pos, tab, g_ref, o_ref, out_ref, ph, plo, w, inv, s_ref, stage, sems):
+    n = NTOP
+    rows = [g_ref.at[i] for i in range(n)] + [o_ref]
+
+    def fetch(i):
+        return pltpu.make_async_copy(rows[i], stage.at[i % 2], sems.at[i % 2])
+
+    fetch(0).start()
+    for i in range(n + 1):
+        if i < n:
+            fetch(i + 1).start()
+        fetch(i).wait()
+        for c in range(4):
+            lo = (c % 2) * H
+            split_into(ph, plo, 2 * i + c // 2, stage[i % 2, c, 0], slice(lo, lo + H))
+            for p in range(2):
+                m = 4 * p + c
+                if m <= i:
+                    for h in range(2):
+                        split_into(ph, plo, xtile(i, m), stage[i % 2, c, 1 + 2 * p + h], slice(h * H, (h + 1) * H))
+
+    def clear(t, _):
+        w[t] = jnp.zeros((B, B), jnp.float32)
+        return 0
+
+    lax.fori_loop(0, NW, clear, 0)
+
+    def product(a, b):
+        return dot3((ph[a], plo[a]), (ph[b], plo[b]))
+
+    for t, a, b, s in first:
+        w[t] = w[t] + s * product(a, b)
+
+    def step(k, _):
+        def task(half, g, i):
+            for u in range(TASKS):
+                if (g % 2) * 8 + i == u * 16 // TASKS:
+                    at = k * slots + half * (slots // 2) + (g // 2) * TASKS + u
+                    t = tab[at, 0]
+                    sign = tab[at, 3].astype(jnp.float32)
+                    w[t] = w[t] + sign * product(tab[at, 1], tab[at, 2])
+
+        d = tri(k, k)
+        u1, v1 = factor_half(s_ref, w[d, :H, :H], functools.partial(task, 0))
+        l21 = small(w[d, H:, :H], v1, NT)
+        u2, v2 = factor_half(s_ref, w[d, H:, H:] - small(l21, l21, NT), functools.partial(task, 1))
+        zero = jnp.zeros((H, H), jnp.float32)
+        inv[:H, :H] = v1
+        inv[:H, H:] = zero
+        inv[H:, :H] = -small(v2, small(l21, v1, NN), NN)
+        inv[H:, H:] = v2
+        w[d, :H, :] = jnp.concatenate([u1.T, zero], axis=1)
+        w[d, H:, :] = jnp.concatenate([l21, u2.T], axis=1)
+        iv = split(inv[...])
+
+        def solve(i, _):
+            t = tri(i, k)
+            x = dot3(split(w[t]), iv)
+            w[t] = x
+            split_into(ph, plo, ltile(i, k), x)
+            return 0
+
+        lax.fori_loop(k + 1, n + 1, solve, 0)
+        t = tri(k + 1, k + 1)
+        a = ltile(k + 1, k)
+        w[t] = w[t] - product(a, a)
+        return 0
+
+    lax.fori_loop(0, n, step, 0)
+    r = pos[0]
+    for p in range(2):
+        m = pos[1] + 4 * p
+        out_ref[0, p] = jnp.where(m <= r, w[jnp.where(m <= r, tri(r, m), 0)], 0.0)
+        out_ref[1, p] = w[tri(n, m)]
+
+
+def run_top(pos, gathered, own):
+    slots = 2 * (H // GRP) * TASKS // 2
+    first, table = plan(slots)
+    any_ = pl.BlockSpec(memory_space=pl.ANY)
+    smem = pl.BlockSpec(memory_space=pltpu.SMEM)
+    return pl.pallas_call(
+        functools.partial(top_kernel, slots, first),
+        out_shape=jax.ShapeDtypeStruct((2, 2, B, B), jnp.float32),
+        in_specs=[smem, smem, any_, any_],
+        out_specs=pl.BlockSpec(memory_space=pltpu.VMEM),
+        scratch_shapes=[
+            pltpu.VMEM((NPOOL, B, B), jnp.bfloat16),
+            pltpu.VMEM((NPOOL, B, B), jnp.bfloat16),
+            pltpu.VMEM((NW, B, B), jnp.float32),
+            pltpu.VMEM((B, B), jnp.float32),
+            pltpu.VMEM((H, 2 * H), jnp.float32),
+            pltpu.VMEM((2, 4, 5, B, H), jnp.float32),
+            pltpu.SemaphoreType.DMA((2,)),
+        ],
+        cost_estimate=pl.CostEstimate(flops=40_000_000_000, bytes_accessed=25_000_000, transcendentals=0),
+        compiler_params=pltpu.CompilerParams(vmem_limit_bytes=58 * 2**20),
+        name="top",
+    )(pos, jnp.asarray(table, jnp.int32), gathered, own)
+
+
+def gather_kernel(x_ref, g_ref, o_ref, zs, zr, xs, xr, ys, yr, cs, cr, ls):
+    r, c = lax.axis_index("row"), lax.axis_index("col")
+    rx = r + 1 - 2 * (r % 2)
+    cy = (c + 2) % 4
+    ck = c + 1 - 2 * (c % 2)
+    nr = 8
+    line = [((r + 2 * d) % nr, c) for d in range(1, 4)]
+    x_dev, y_dev, k_dev = (rx, c), (r, cy), (r, ck)
+
+    barrier = pltpu.get_barrier_semaphore()
+    for dev in line + [x_dev, y_dev, k_dev]:
+        pl.semaphore_signal(barrier, inc=1, device_id=dev, device_id_type=pl.DeviceIdType.MESH)
+    pl.semaphore_wait(barrier, 6)
+
+    def copy(src, dst, dev, ssem, rsem):
+        return pltpu.make_async_remote_copy(
+            src_ref=src, dst_ref=dst, send_sem=ssem, recv_sem=rsem, device_id=dev, device_id_type=pl.DeviceIdType.MESH
+        )
+
+    def each(piece, act):
+        i, j = piece
+        for n, cond in ((1, i < j), (3, (i >= j) & (i < 4 + j)), (5, i >= 4 + j)):
+            pl.when(cond)(functools.partial(act, n))
+
+    sent = []
+
+    def send(piece, dev, ssem, rsem, mine=False):
+        i, j = piece
+
+        def make(n):
+            src = x_ref.at[0, pl.ds(0, n)] if mine else g_ref.at[i, j, pl.ds(0, n)]
+            return copy(src, g_ref.at[i, j, pl.ds(0, n)], dev, ssem, rsem)
+
+        each(piece, lambda n: make(n).start())
+        sent.append((piece, lambda n: make(n).wait_send()))
+
+    def arrived(piece, rsem):
+        i, j = piece
+        at = lambda n: g_ref.at[i, j, pl.ds(0, n)]
+        each(piece, lambda n: copy(at(n), at(n), k_dev, cs.at[0], rsem).wait_recv())
+
+    keep = [
+        pltpu.make_async_copy(x_ref.at[0], g_ref.at[r, c], ls.at[0]),
+        pltpu.make_async_copy(x_ref.at[1], o_ref.at[c], ls.at[1]),
+    ]
+    for d in range(3):
+        send((r, c), line[d], zs.at[d], zr.at[d], True)
+    send((r, c), x_dev, xs.at[0], xr.at[0], True)
+    send((r, c), y_dev, ys.at[0], yr.at[0], True)
+    send((r, c), k_dev, cs.at[0], cr.at[0], True)
+    for cp in keep:
+        cp.start()
+    low = [
+        copy(x_ref.at[1], o_ref.at[c], y_dev, ys.at[6], yr.at[6]),
+        copy(x_ref.at[1], o_ref.at[c], k_dev, cs.at[16], cr.at[16]),
+        copy(o_ref.at[cy], o_ref.at[cy], k_dev, cs.at[17], cr.at[17]),
+    ]
+    low[0].start()
+    low[1].start()
+    for d in range(1, 4):
+        p = ((r + nr - 2 * d) % nr, c)
+        arrived(p, zr.at[d - 1])
+        send(p, x_dev, xs.at[d], xr.at[d])
+        send(p, y_dev, ys.at[d], yr.at[d])
+        send(p, k_dev, cs.at[d], cr.at[d])
+    for s in range(4):
+        px = ((rx + nr - 2 * s) % nr, c)
+        arrived(px, xr.at[s])
+        if s % 2:
+            send(px, y_dev, ys.at[4 + s // 2], yr.at[4 + s // 2])
+        send(px, k_dev, cs.at[4 + s], cr.at[4 + s])
+        py = ((r + nr - 2 * s) % nr, cy)
+        arrived(py, yr.at[s])
+        if s % 2 == 0:
+            send(py, x_dev, xs.at[4 + s // 2], xr.at[4 + s // 2])
+        send(py, k_dev, cs.at[8 + s], cr.at[8 + s])
+    low[0].wait_recv()
+    low[2].start()
+    for s in range(4):
+        pd = ((rx + nr - 2 * s) % nr, cy)
+        arrived(pd, (yr if s % 2 else xr).at[4 + s // 2])
+        send(pd, k_dev, cs.at[12 + s], cr.at[12 + s])
+    cky = (ck + 2) % 4
+    for t, (i, j) in enumerate(((r, ck), (rx, ck), (r, cky), (rx, cky))):
+        for s in range(4):
+            arrived(((i + nr - 2 * s) % nr, j), cr.at[4 * t + s])
+    low[1].wait_recv()
+    low[2].wait_recv()
+    for piece, done in sent:
+        each(piece, done)
+    for cp in low:
+        cp.wait_send()
+    for cp in keep:
+        cp.wait()
+
+
+def gather_rows(x):
+    tile = x.shape[1:]
+    dma = lambda n: pltpu.SemaphoreType.DMA((n,))
+    any_ = pl.BlockSpec(memory_space=pl.ANY)
+    return pl.pallas_call(
+        gather_kernel,
+        out_shape=[jax.ShapeDtypeStruct((8, 4, *tile), x.dtype), jax.ShapeDtypeStruct((4, *tile), x.dtype)],
+        in_specs=[any_],
+        out_specs=[any_, any_],
+        scratch_shapes=[dma(3), dma(3), dma(6), dma(6), dma(7), dma(7), dma(18), dma(18), dma(2)],
+        compiler_params=pltpu.CompilerParams(collective_id=0, has_side_effects=True),
+        name="gather",
+    )(x)
 
 
 def run_panel(p, idx, ntile, nown, sizes, *arrays):
@@ -203,6 +463,11 @@
     nr, nc = lax.axis_size("row"), lax.axis_size("col")
     r, c = lax.axis_index("row"), lax.axis_index("col")
     ntile = PANELS * PANEL // tile_rows
+    if (nr, nc, blocks, panels, tile_rows, tc, uc) == (NTOP, 4, 2, 2, B, B, H):
+        x = factor.reshape(2, B, 4, H).transpose(0, 2, 1, 3)
+        x = jnp.concatenate([update[:, None], x], axis=1)
+        idx = jnp.stack([r, c]).astype(jnp.int32)
+        return run_top(idx, *gather_rows(x)).transpose(0, 2, 1, 3)
     whole_rows = nr == ntile
     nown = blocks - 1 if whole_rows else blocks
     sizes = (tc, uc, nc)

time: 307 us -> 218 us (0.71)
  waiting for transfers between devices: 118 us -> 0 us
  Pallas kernels: 150 us -> 211 us
  between operations: 14.4 us -> 0.04 us
  local copies, waits for them, and re-layouts: 18.4 us -> 5.41 us
    all_gather x4 -> x0, waiting for transfers between devices: 118 us -> none  [the longest x2 97.1 us: diag(): return lax.all_gather(x, ('row', 'col')).reshape(ntile, nc, *x.shape)]
    pallas_call x2, Pallas kernels: 150 us -> 211 us  [the longest x1 109 us: run_top(): pl.pallas_call(functools.partial(top_kernel, slots, first), out_shape=jax...]
    slice x6 -> x0, local copies, waits for them, and re-layouts: 16.6 us -> none  [the longest x1 6.3 us: per_device(): da[ntile // 2:]]
  transfers between devices with their start and end apart: 4 -> 0, of which waited for: 2 -> 0; matrix products, arithmetic and copies ran while one was open for 4% -> 0% of each run, Pallas kernels for 27% -> 0%
where the time goes in v2:
time: 218 us
  Pallas kernels  211 us (97%)
  local copies, waits for them, and re-layouts  5.41 us (2%)
    pallas_call x1, Pallas kernels, run_top(): pl.pallas_call(functools.partial(top_kernel, slots, first), out_shape=jax...  109 us
    pallas_call x1, Pallas kernels, gather_rows(): pl.pallas_call(gather_kernel, out_shape=[jax.ShapeDtypeStruct((8, 4, *til...  102 us

profile of v2, /device:TPU:9, one launch (start us, length us, event | category | flops | bytes accessed | tf_op | source)
XLA Modules:
  0.0 218.2 jit_solution(4906279007475488661)
XLA Ops:
  0.0 0.6 pad_add_fusion.pos
  0.6 1.5 copy.5
  2.1 0.0 copy-start
  2.1 0.3 copy.6
  2.4 0.6 copy-done
  3.0 1.2 pad_maximum_fusion.x_ref
  4.2 102.4 %gather.1 = (f32[8,4,5,256,128]{4,3,2,1,0:T(8,128)}, f32[4,5,256,128]{3,2,1,0:T(8,128)}) custom-call(f32[2,5,256,128]{3,2,1,0:T(8,128)} %pad_maximum_fusion.x_ref), custom_call_target="tpu_custom_call" | custom-call | tf_op jit(solution)/shard_map/gather/pallas_call | solution.py:420
  106.6 108.6 %top.1 = f32[2,2,256,256]{3,2,1,0:T(8,128)} custom-call(s32[2]{0:T(128)} %pad_add_fusion.pos, s32[384,4]{1,0:T(8,128)} %constant.11.clone.tab, f32[8,4,5,256,128]{4,3,2,1,0:T(8,128)} %get-tuple-element.7.g_ref, f32[4,5,256,128]{3,2,1,0:T(8,128)} %get-tuple-element.8.o_ref), custom_call_target="tpu_custom_call" | custom-call | flops 40000000000 | bytes 25000000 | tf_op jit(solution)/shard_map/top/pallas_call | solution.py:300
  215.2 3.0 %copy.7 = f32[2,256,2,256]{3,2,1,0:T(2,128)} copy(f32[2,256,2,256]{3,1,2,0:T(8,128)} %bitcast.8) | data formatting | bytes 2097152 | tf_op jit(solution)/shard_map/transpose | solution.py:470
Async XLA Ops:
  2.1 1.0 copy-start

commit v3 on v2

--- a/solution.py
+++ b/solution.py
@@ -171,6 +171,7 @@
 
 
 TASKS = 3
+BATCH = 3
 NTOP = 8
 
 
@@ -187,7 +188,7 @@
 
 
 NW = tri(NTOP, NTOP) + 1
-NPOOL = ltile(NTOP, NTOP)
+NPOOL = ltile(NTOP, NTOP) + 1
 
 
 def plan(slots, late=()):
@@ -218,30 +219,33 @@
 
 def top_kernel(slots, first, pos, tab, g_ref, o_ref, out_ref, ph, plo, w, inv, s_ref, stage, sems):
     n = NTOP
-    rows = [g_ref.at[i] for i in range(n)] + [o_ref]
+    deep = 3
 
     def fetch(i):
-        return pltpu.make_async_copy(rows[i], stage.at[i % 2], sems.at[i % 2])
-
-    fetch(0).start()
+        m = 3 if i < n // 2 else 5
+        src = o_ref if i == n else g_ref.at[i, :, pl.ds(0, m)]
+        return pltpu.make_async_copy(src, stage.at[i % deep, :, pl.ds(0, m)], sems.at[i % deep])
+
+    for i in range(deep - 1):
+        fetch(i).start()
+
+    def clear(t, _):
+        w[t] = jnp.zeros((B, B), jnp.float32)
+        return 0
+
+    lax.fori_loop(0, NW, clear, 0)
     for i in range(n + 1):
-        if i < n:
-            fetch(i + 1).start()
+        if i + deep - 1 <= n:
+            fetch(i + deep - 1).start()
         fetch(i).wait()
         for c in range(4):
             lo = (c % 2) * H
-            split_into(ph, plo, 2 * i + c // 2, stage[i % 2, c, 0], slice(lo, lo + H))
+            split_into(ph, plo, 2 * i + c // 2, stage[i % deep, c, 0], slice(lo, lo + H))
             for p in range(2):
                 m = 4 * p + c
                 if m <= i:
                     for h in range(2):
-                        split_into(ph, plo, xtile(i, m), stage[i % 2, c, 1 + 2 * p + h], slice(h * H, (h + 1) * H))
-
-    def clear(t, _):
-        w[t] = jnp.zeros((B, B), jnp.float32)
-        return 0
-
-    lax.fori_loop(0, NW, clear, 0)
+                        split_into(ph, plo, xtile(i, m), stage[i % deep, c, 1 + 2 * p + h], slice(h * H, (h + 1) * H))
 
     def product(a, b):
         return dot3((ph[a], plo[a]), (ph[b], plo[b]))
@@ -271,14 +275,22 @@
         w[d, H:, :] = jnp.concatenate([l21, u2.T], axis=1)
         iv = split(inv[...])
 
-        def solve(i, _):
-            t = tri(i, k)
-            x = dot3(split(w[t]), iv)
-            w[t] = x
-            split_into(ph, plo, ltile(i, k), x)
+        def solve(u, _):
+            at, to, x = [], [], []
+            for v in range(BATCH):
+                i = k + 1 + BATCH * u + v
+                spare = (i > n).astype(jnp.int32) if v else 0
+                i = i - spare * (i - n)
+                at.append(tri(i, k) + spare * (NW - 1 - tri(n, k)) if v else tri(i, k))
+                to.append(ltile(i, k) + spare * (NPOOL - 1 - ltile(n, k)) if v else ltile(i, k))
+                x.append(split(w[at[v]]))
+            x = [dot3(y, iv) for y in x]
+            for v in range(BATCH):
+                w[at[v]] = x[v]
+                split_into(ph, plo, to[v], x[v])
             return 0
 
-        lax.fori_loop(k + 1, n + 1, solve, 0)
+        lax.fori_loop(0, (n - k + BATCH - 1) // BATCH, solve, 0)
         t = tri(k + 1, k + 1)
         a = ltile(k + 1, k)
         w[t] = w[t] - product(a, a)
@@ -308,8 +320,8 @@
             pltpu.VMEM((NW, B, B), jnp.float32),
             pltpu.VMEM((B, B), jnp.float32),
             pltpu.VMEM((H, 2 * H), jnp.float32),
-            pltpu.VMEM((2, 4, 5, B, H), jnp.float32),
-            pltpu.SemaphoreType.DMA((2,)),
+            pltpu.VMEM((3, 4, 5, B, H), jnp.float32),
+            pltpu.SemaphoreType.DMA((3,)),
         ],
         cost_estimate=pl.CostEstimate(flops=40_000_000_000, bytes_accessed=25_000_000, transcendentals=0),
         compiler_params=pltpu.CompilerParams(vmem_limit_bytes=58 * 2**20),

time: 218 us -> 211 us (0.968)
  Pallas kernels: 211 us -> 203 us
    pallas_call x1, Pallas kernels: 109 us -> 101 us  [run_top(): pl.pallas_call(functools.partial(top_kernel, slots, first), out_shape=jax...]
where the time goes in v3:
time: 211 us; the launch traced here: 210 us
  Pallas kernels  203 us (96%)
  local copies, waits for them, and re-layouts  5.41 us (3%)
    pallas_call x1, Pallas kernels, gather_rows(): pl.pallas_call(gather_kernel, out_shape=[jax.ShapeDtypeStruct((8, 4, *til...  102 us
    pallas_call x1, Pallas kernels, run_top(): pl.pallas_call(functools.partial(top_kernel, slots, first), out_shape=jax...  101 us

profile of v3, /device:TPU:9, one launch (start us, length us, event | category | flops | bytes accessed | tf_op | source)
XLA Modules:
  0.0 210.4 jit_solution(12703673579119009235)
XLA Ops:
  0.0 0.6 pad_add_fusion.pos
  0.6 1.5 copy.5
  2.1 0.0 copy-start
  2.1 0.3 copy.6
  2.4 0.6 copy-done
  3.0 1.2 pad_maximum_fusion.x_ref
  4.2 102.4 %gather.1 = (f32[8,4,5,256,128]{4,3,2,1,0:T(8,128)}, f32[4,5,256,128]{3,2,1,0:T(8,128)}) custom-call(f32[2,5,256,128]{3,2,1,0:T(8,128)} %pad_maximum_fusion.x_ref), custom_call_target="tpu_custom_call" | custom-call | tf_op jit(solution)/shard_map/gather/pallas_call | solution.py:432
  106.6 100.8 %top.1 = f32[2,2,256,256]{3,2,1,0:T(8,128)} custom-call(s32[2]{0:T(128)} %pad_add_fusion.pos, s32[384,4]{1,0:T(8,128)} %constant.11.clone.tab, f32[8,4,5,256,128]{4,3,2,1,0:T(8,128)} %get-tuple-element.7.g_ref, f32[4,5,256,128]{3,2,1,0:T(8,128)} %get-tuple-element.8.o_ref), custom_call_target="tpu_custom_call" | custom-call | flops 40000000000 | bytes 25000000 | tf_op jit(solution)/shard_map/top/pallas_call | solution.py:312
  207.4 3.0 %copy.7 = f32[2,256,2,256]{3,2,1,0:T(2,128)} copy(f32[2,256,2,256]{3,1,2,0:T(8,128)} %bitcast.8) | data formatting | bytes 2097152 | tf_op jit(solution)/shard_map/transpose | solution.py:482
Async XLA Ops:
  2.1 1.0 copy-start

commit v4 on v3

--- a/solution.py
+++ b/solution.py
@@ -271,8 +271,8 @@
         inv[:H, H:] = zero
         inv[H:, :H] = -small(v2, small(l21, v1, NN), NN)
         inv[H:, H:] = v2
-        w[d, :H, :] = jnp.concatenate([u1.T, zero], axis=1)
-        w[d, H:, :] = jnp.concatenate([l21, u2.T], axis=1)
+        w[d, :H, :H] = u1
+        w[d, H:, :] = jnp.concatenate([l21, u2], axis=1)
         iv = split(inv[...])
 
         def solve(u, _):
@@ -298,10 +298,16 @@
 
     lax.fori_loop(0, n, step, 0)
     r = pos[0]
+    zero = jnp.zeros((H, H), jnp.float32)
     for p in range(2):
         m = pos[1] + 4 * p
-        out_ref[0, p] = jnp.where(m <= r, w[jnp.where(m <= r, tri(r, m), 0)], 0.0)
-        out_ref[1, p] = w[tri(n, m)]
+        x = jnp.where(m <= r, w[jnp.where(m <= r, tri(r, m), 0)], 0.0)
+        turned = jnp.concatenate(
+            [jnp.concatenate([x[:H, :H].T, zero], axis=1), jnp.concatenate([x[H:, :H], x[H:, H:].T], axis=1)], axis=0
+        )
+        for e, y in enumerate((jnp.where(m == r, turned, x), w[tri(n, m)])):
+            for h in range(2):
+                out_ref[pl.ds(4 * B * e + 2 * h + p, B, stride=4), :] = y[:, h * H : (h + 1) * H]
 
 
 def run_top(pos, gathered, own):
@@ -311,7 +317,7 @@
     smem = pl.BlockSpec(memory_space=pltpu.SMEM)
     return pl.pallas_call(
         functools.partial(top_kernel, slots, first),
-        out_shape=jax.ShapeDtypeStruct((2, 2, B, B), jnp.float32),
+        out_shape=jax.ShapeDtypeStruct((8 * B, H), jnp.float32),
         in_specs=[smem, smem, any_, any_],
         out_specs=pl.BlockSpec(memory_space=pltpu.VMEM),
         scratch_shapes=[
@@ -479,7 +485,8 @@
         x = factor.reshape(2, B, 4, H).transpose(0, 2, 1, 3)
         x = jnp.concatenate([update[:, None], x], axis=1)
         idx = jnp.stack([r, c]).astype(jnp.int32)
-        return run_top(idx, *gather_rows(x)).transpose(0, 2, 1, 3)
+        out = run_top(idx, *gather_rows(x)).reshape(2, B, 2, 2, H)
+        return out.transpose(0, 1, 3, 2, 4).reshape(2, B, 2, 2 * H)
     whole_rows = nr == ntile
     nown = blocks - 1 if whole_rows else blocks
     sizes = (tc, uc, nc)

time: 211 us -> 208 us (0.986)
  local copies, waits for them, and re-layouts: 5.41 us -> 2.4 us
    transpose x1 -> x0, local copies, waits for them, and re-layouts: 3 us -> none  [per_device(): return run_top(idx, *gather_rows(x)).transpose(0, 2, 1, 3)]
where the time goes in v4:
time: 208 us; the launch traced here: 207 us
  Pallas kernels  203 us (98%)
  local copies, waits for them, and re-layouts  2.4 us (1%)
    pallas_call x1, Pallas kernels, gather_rows(): pl.pallas_call(gather_kernel, out_shape=[jax.ShapeDtypeStruct((8, 4, *til...  102 us
    pallas_call x1, Pallas kernels, run_top(): pl.pallas_call(functools.partial(top_kernel, slots, first), out_shape=jax...  101 us

profile of v4, /device:TPU:9, one launch (start us, length us, event | category | flops | bytes accessed | tf_op | source)
XLA Modules:
  0.0 207.5 jit_solution(15279781672769099520)
XLA Ops:
  0.0 0.6 pad_add_fusion.pos
  0.6 1.5 copy.5
  2.1 0.0 copy-start
  2.1 0.3 copy.6
  2.4 0.6 copy-done
  3.0 1.2 pad_maximum_fusion.x_ref
  4.2 102.4 %gather.1 = (f32[8,4,5,256,128]{4,3,2,1,0:T(8,128)}, f32[4,5,256,128]{3,2,1,0:T(8,128)}) custom-call(f32[2,5,256,128]{3,2,1,0:T(8,128)} %pad_maximum_fusion.x_ref), custom_call_target="tpu_custom_call" | custom-call | tf_op jit(solution)/shard_map/gather/pallas_call | solution.py:438
  106.6 100.8 %top.1 = f32[2048,128]{1,0:T(8,128)} custom-call(s32[2]{0:T(128)} %pad_add_fusion.pos, s32[384,4]{1,0:T(8,128)} %constant.11.clone.tab, f32[8,4,5,256,128]{4,3,2,1,0:T(8,128)} %get-tuple-element.7.g_ref, f32[4,5,256,128]{3,2,1,0:T(8,128)} %get-tuple-element.8.o_ref), custom_call_target="tpu_custom_call" | custom-call | flops 40000000000 | bytes 25000000 | tf_op jit(solution)/shard_map/top/pallas_call | solution.py:318
Async XLA Ops:
  2.1 1.0 copy-start
